TPU v7x, 32 devices: a whole 2x2x4 slice. The times are simulated.
32 devices in a mesh: blk: 2 (over y), dp: 16 (over z, x, core).
Axes of the slice: x: 2, y: 2, z: 4, core: 2. Of those that a mesh axis runs over, the one named last changes fastest.
Arguments:
- tokens: bfloat16 [16, 454, 768], P('dp', 'blk'), may hold values from -6 to 6
- segment_ids: int32 [16, 454], P('dp'), may hold values from 0 to 5, as said below
- expert_ids: int32 [16, 454], P('dp'), may hold values from 0 to 2, as said below
- norm_first: float32 [768], replicated, may hold values from 0.5 to 1.5
- project_in: bfloat16 [768, 2304], replicated, may hold values from -0.21875 to 0.21875
- project_out: bfloat16 [768, 768], replicated, may hold values from -2 to 2
- norm_second: float32 [768], replicated, may hold values from 0.5 to 1.5
- up_weight: bfloat16 [3, 768, 3072], P(None, None, 'blk'), may hold values from -0.21875 to 0.21875
- down_weight: bfloat16 [3, 3072, 768], P(None, 'blk'), may hold values from -0.109375 to 0.109375
- cotangent: bfloat16 [16, 454, 768], P('dp', 'blk'), may hold values from -6 to 6
Outputs:
- layer_out: bfloat16 [16, 454, 768], P('dp', 'blk')
- input_grad: bfloat16 [16, 454, 768], P('dp', 'blk')
- grad_norm_first: float32 [768], P('dp')
- grad_project_in: float32 [768, 2304], P('dp')
- grad_project_out: float32 [768, 768], P('dp')
- grad_norm_second: float32 [768], P('dp')
- grad_up: float32 [3, 768, 3072], P(None, 'dp', 'blk')
- grad_down: float32 [3, 3072, 768], P(None, 'blk', 'dp')
Inputs may be any that keep to these rules, and one draw needn't show every extreme that they name: `segment_ids`: each group holds some whole captions numbered 1 upward, then its 197 image tokens (id 0), which take the last slots of the first 227 and the first slots of the rest, then its remaining captions numbered on; every caption has 1 to 64 tokens and caption 1 has 64. `expert_ids`: the same for all tokens of one image or one caption; an image's tokens use expert 0 or 2, a caption's expert 1 or 2.
All inputs are finite; a program needn't handle non-finite values.
Results may differ from a plain program's by a relative error of at most 0.015.
Values may be sent and summed in bfloat16 or wider, within the bound.
No kernel may reach another device: no remote copies, remote signals or barrier semaphores. Data moves between devices by JAX's collectives and lax.ppermute only.
A program may use at most 256 MiB of HBM per device.

v0:
```python
import jax
import jax.numpy as jnp
from jax import lax
from jax.sharding import PartitionSpec as P

HEADS = 12
HEAD_DIM = 64
EXPERTS = 3


EPSILON = 1e-05
NEGATIVE = -1e30
ROOT_HALF = 0.7071067811865476
INV_ROOT_TAU = 0.3989422804014327


def passed_along(value, axis, steps):
    count = lax.axis_size(axis)
    pairs = [(source, (source + steps) % count) for source in range(count)]
    return lax.ppermute(value, axis, pairs)


def layer_norm(values, gain):
    row_mean = jnp.mean(values, axis=-1, keepdims=True)
    centred = values - row_mean
    row_var = jnp.mean(centred * centred, axis=-1, keepdims=True)
    return centred * lax.rsqrt(row_var + EPSILON) * gain


def gelu_value(upward):
    return 0.5 * upward * (1.0 + lax.erf(upward * ROOT_HALF))


def gelu_slope(upward):
    return 0.5 * (1.0 + lax.erf(upward * ROOT_HALF)) + upward * INV_ROOT_TAU * jnp.exp(
        -0.5 * upward * upward
    )


def allowed_mask(segment_query, segment_key):
    return (segment_key[None, :] == 0) | (segment_key[None, :] == segment_query[:, None])


def head_scores(queries, key_rows, allowed):
    raw_scores = jnp.einsum(
        "qhd,khd->hqk", queries, key_rows, preferred_element_type=jnp.float32
    ) * HEAD_DIM ** (-0.5)
    return jnp.where(allowed[None], raw_scores, NEGATIVE)


def expert_forward(normed_rows, onehot, weight_up, weight_down):
    upward = jnp.einsum("rd,edf->erf", normed_rows, weight_up, preferred_element_type=jnp.float32)
    active = (gelu_value(upward) * onehot.T[:, :, None]).astype(jnp.bfloat16)
    branch = jnp.einsum("erf,efd->rd", active, weight_down, preferred_element_type=jnp.float32)
    return (upward, active, branch)


def expert_backward(normed_rows, onehot, weight_up, weight_down, upward, active, grad_rows):
    grad_active = (
        jnp.einsum("rd,efd->erf", grad_rows, weight_down, preferred_element_type=jnp.float32)
        * onehot.T[:, :, None]
    )
    grad_upward = (grad_active * gelu_slope(upward)).astype(jnp.bfloat16)
    grad_down_part = jnp.einsum(
        "erf,rd->def", active, grad_rows, preferred_element_type=jnp.float32
    )
    grad_up_part = jnp.einsum(
        "rd,erf->def", normed_rows, grad_upward, preferred_element_type=jnp.float32
    )
    grad_normed = jnp.einsum(
        "erf,edf->rd", grad_upward, weight_up, preferred_element_type=jnp.float32
    )
    return (grad_normed, grad_up_part, grad_down_part)


def body(
    tokens,
    segment_ids,
    expert_ids,
    norm_first,
    project_in,
    project_out,
    norm_second,
    up_weight,
    down_weight,
    cotangent,
):
    row_count = tokens.shape[1]
    width = tokens.shape[2]
    own_rows = tokens[0].astype(jnp.float32)
    position = lax.axis_index("blk")
    own_start = position * row_count
    other_start = (1 - position) * row_count
    segment_all = segment_ids[0]
    segment_own = lax.dynamic_slice_in_dim(segment_all, own_start, row_count)
    segment_other = lax.dynamic_slice_in_dim(segment_all, other_start, row_count)
    near_mask = allowed_mask(segment_own, segment_own)
    far_mask = allowed_mask(segment_own, segment_other)
    normed, norm_pull = jax.vjp(layer_norm, own_rows, norm_first)
    normed_low = normed.astype(jnp.bfloat16)
    projected = jnp.dot(normed_low, project_in, preferred_element_type=jnp.float32).astype(
        jnp.bfloat16
    )
    queries = projected[:, :width].reshape(row_count, HEADS, HEAD_DIM)
    keys_values = projected[:, width:]
    key_rows = keys_values[:, :width].reshape(row_count, HEADS, HEAD_DIM)
    value_rows = keys_values[:, width:].reshape(row_count, HEADS, HEAD_DIM)
    far_pairs = passed_along(keys_values, "blk", 1)
    far_keys = far_pairs[:, :width].reshape(row_count, HEADS, HEAD_DIM)
    far_values = far_pairs[:, width:].reshape(row_count, HEADS, HEAD_DIM)
    near_scores = head_scores(queries, key_rows, near_mask)
    far_scores = head_scores(queries, far_keys, far_mask)
    row_peak = jnp.maximum(jnp.max(near_scores, axis=-1), jnp.max(far_scores, axis=-1))
    near_raised = jnp.exp(near_scores - row_peak[..., None])
    far_raised = jnp.exp(far_scores - row_peak[..., None])
    row_total = jnp.sum(near_raised, axis=-1) + jnp.sum(far_raised, axis=-1)
    log_total = row_peak + jnp.log(row_total)
    near_weight = (near_raised / row_total[..., None]).astype(jnp.bfloat16)
    far_weight = (far_raised / row_total[..., None]).astype(jnp.bfloat16)
    heads_out = jnp.einsum(
        "hqk,khd->qhd", near_weight, value_rows, preferred_element_type=jnp.float32
    )
    heads_out = heads_out + jnp.einsum(
        "hqk,khd->qhd", far_weight, far_values, preferred_element_type=jnp.float32
    )
    attended = heads_out.reshape(row_count, width).astype(jnp.bfloat16)
    middle = own_rows + jnp.dot(attended, project_out, preferred_element_type=jnp.float32)
    normed_two, norm_two_pull = jax.vjp(layer_norm, middle, norm_second)
    normed_two_low = normed_two.astype(jnp.bfloat16)
    onehot_all = (expert_ids[0][:, None] == jnp.arange(EXPERTS, dtype=jnp.int32)[None, :]).astype(
        jnp.float32
    )
    grad_out = cotangent[0]
    gathered = lax.all_gather(normed_two_low, "blk", axis=0, tiled=True)
    upward, active, partial_out = expert_forward(gathered, onehot_all, up_weight, down_weight)
    expert_out = lax.psum_scatter(
        partial_out.astype(jnp.bfloat16), "blk", scatter_dimension=0, tiled=True
    ).astype(jnp.float32)
    grad_gathered = lax.all_gather(grad_out, "blk", axis=0, tiled=True)
    grad_partial, grad_up_part, grad_down_part = expert_backward(
        gathered, onehot_all, up_weight, down_weight, upward, active, grad_gathered
    )
    grad_normed_two = lax.psum_scatter(
        grad_partial.astype(jnp.bfloat16), "blk", scatter_dimension=0, tiled=True
    ).astype(jnp.float32)
    rows_up, rows_down = (
        lax.psum_scatter(grad_up_part, "dp", scatter_dimension=0, tiled=True),
        lax.psum_scatter(grad_down_part, "dp", scatter_dimension=0, tiled=True),
    )
    grad_up_out = jnp.transpose(rows_up, (1, 0, 2))
    grad_down_out = jnp.transpose(rows_down, (1, 2, 0))
    layer_out = (middle + expert_out).astype(jnp.bfloat16)[None]
    grad_middle_norm, grad_gain_two = norm_two_pull(grad_normed_two)
    grad_middle = grad_out.astype(jnp.float32) + grad_middle_norm
    grad_branch = grad_middle.astype(jnp.bfloat16)
    grad_out_part = jnp.einsum(
        "rd,re->de", attended, grad_branch, preferred_element_type=jnp.float32
    )
    grad_attended = jnp.einsum(
        "re,de->rd", grad_branch, project_out, preferred_element_type=jnp.float32
    ).astype(jnp.bfloat16)
    grad_attended = grad_attended.reshape(row_count, HEADS, HEAD_DIM)
    back_pairs = passed_along(keys_values, "blk", 1)
    back_keys = back_pairs[:, :width].reshape(row_count, HEADS, HEAD_DIM)
    back_values = back_pairs[:, width:].reshape(row_count, HEADS, HEAD_DIM)
    near_scores = head_scores(queries, key_rows, near_mask)
    far_scores = head_scores(queries, back_keys, far_mask)
    near_prob = jnp.exp(near_scores - log_total[..., None])
    far_prob = jnp.exp(far_scores - log_total[..., None])
    near_dprob = jnp.einsum(
        "qhd,khd->hqk", grad_attended, value_rows, preferred_element_type=jnp.float32
    )
    far_dprob = jnp.einsum(
        "qhd,khd->hqk", grad_attended, back_values, preferred_element_type=jnp.float32
    )
    delta = jnp.sum(near_prob * near_dprob, axis=-1) + jnp.sum(far_prob * far_dprob, axis=-1)
    near_dscore = (near_prob * (near_dprob - delta[..., None])).astype(jnp.bfloat16)
    far_dscore = (far_prob * (far_dprob - delta[..., None])).astype(jnp.bfloat16)
    score_scale = HEAD_DIM ** (-0.5)
    grad_queries = jnp.einsum(
        "hqk,khd->qhd", near_dscore, key_rows, preferred_element_type=jnp.float32
    )
    grad_queries = grad_queries + jnp.einsum(
        "hqk,khd->qhd", far_dscore, back_keys, preferred_element_type=jnp.float32
    )
    grad_queries = (grad_queries * score_scale).astype(jnp.bfloat16).reshape(row_count, width)
    near_grad_keys = (
        jnp.einsum("hqk,qhd->khd", near_dscore, queries, preferred_element_type=jnp.float32)
        * score_scale
    )
    near_grad_values = jnp.einsum(
        "hqk,qhd->khd",
        near_prob.astype(jnp.bfloat16),
        grad_attended,
        preferred_element_type=jnp.float32,
    )
    far_grad_keys = (
        jnp.einsum("hqk,qhd->khd", far_dscore, queries, preferred_element_type=jnp.float32)
        * score_scale
    )
    far_grad_values = jnp.einsum(
        "hqk,qhd->khd",
        far_prob.astype(jnp.bfloat16),
        grad_attended,
        preferred_element_type=jnp.float32,
    )
    far_grads = jnp.concatenate(
        [far_grad_keys.reshape(row_count, width), far_grad_values.reshape(row_count, width)], axis=1
    )
    returned = passed_along(far_grads.astype(jnp.bfloat16), "blk", 1).astype(far_grads.dtype)
    near_grads = jnp.concatenate(
        [near_grad_keys.reshape(row_count, width), near_grad_values.reshape(row_count, width)],
        axis=1,
    )
    landed = near_grads + returned
    near_grads = landed
    grad_pairs = near_grads.astype(jnp.bfloat16)
    grad_projected = jnp.concatenate([grad_queries, grad_pairs], axis=1)
    grad_in_part = jnp.einsum(
        "rd,re->de", normed_low, grad_projected, preferred_element_type=jnp.float32
    )
    grad_normed = jnp.einsum(
        "re,de->rd", grad_projected, project_in, preferred_element_type=jnp.float32
    )
    grad_rows_norm, grad_gain_one = norm_pull(grad_normed)
    input_grad = (grad_middle + grad_rows_norm).astype(jnp.bfloat16)[None]
    summed_dp = (
        lax.psum_scatter(grad_gain_one, "dp", scatter_dimension=0, tiled=True),
        lax.psum_scatter(grad_in_part, "dp", scatter_dimension=0, tiled=True),
        lax.psum_scatter(grad_out_part, "dp", scatter_dimension=0, tiled=True),
        lax.psum_scatter(grad_gain_two, "dp", scatter_dimension=0, tiled=True),
    )
    gain_one_out, in_out, out_out, gain_two_out = (
        lax.psum(summed_dp[0].astype(jnp.bfloat16), "blk").astype(jnp.float32),
        lax.psum(summed_dp[1].astype(jnp.bfloat16), "blk").astype(jnp.float32),
        lax.psum(summed_dp[2].astype(jnp.bfloat16), "blk").astype(jnp.float32),
        lax.psum(summed_dp[3].astype(jnp.bfloat16), "blk").astype(jnp.float32),
    )
    return (
        layer_out,
        input_grad,
        gain_one_out,
        in_out,
        out_out,
        gain_two_out,
        grad_up_out,
        grad_down_out,
    )


def solution(mesh):
    return jax.shard_map(
        body,
        mesh=mesh,
        in_specs=(
            P("dp", "blk", None),
            P("dp", None),
            P("dp", None),
            P(),
            P(),
            P(),
            P(),
            P(None, None, "blk"),
            P(None, "blk", None),
            P("dp", "blk", None),
        ),
        out_specs=(
            P("dp", "blk", None),
            P("dp", "blk", None),
            P("dp"),
            P("dp", None),
            P("dp", None),
            P("dp"),
            P(None, "dp", "blk"),
            P(None, "blk", "dp"),
        ),
        check_vma=False,
    )
```

profile of v0, /device:TPU:0, one launch (start us, length us, event | category | flops | bytes accessed | tf_op | source)
XLA Modules:
  0.0 840.6 jit_solution(5526887371314874461)
XLA Ops:
  13.3 3.0 collective-permute-start
  23.6 2.4 copy.87
  26.0 22.7 %all-gather = bf16[1,454,768]{2,0,1:T(2,128)(2,1)} all-gather(bf16[1,227,768]{2,0,1:T(2,128)(2,1)} %copy.87), channel_id=2, replica_groups=mesh['blk'=2,'dp'=16] {'blk'}, dimensions={1}, use_global_device_ids=true | all-gather | bytes 1046016 | tf_op jit(solution)/shard_map/all_gather | solution.py:139
  49.6 3.3 fusion.72
  66.5 10.4 %all-gather.1 = bf16[2,227,768]{2,1,0:T(8,128)(2,1)} all-gather(bf16[1,227,768]{2,1,0:T(8,128)(2,1)S(1)} %fusion.55), channel_id=1, replica_groups=mesh['blk'=2,'dp'=16] {'blk'}, dimensions={0}, use_global_device_ids=true | all-gather | bytes 1046016 | tf_op jit(solution)/shard_map/all_gather | solution.py:134
  79.1 6.3 fusion.9
  85.4 8.1 fusion.25
  93.5 7.9 fusion.6
  103.4 4.3 fusion.26
  107.7 19.7 %fusion.68 = (bf16[232,768]{1,0:T(8,128)(2,1)}, bf16[232,768]{1,0:T(8,128)(2,1)}) fusion(bf16[454,768]{1,0:T(8,128)(2,1)} %fusion.25, bf16[454,768]{1,0:T(8,128)(2,1)} %fusion.26), kind=kCustom, calls=%all-reduce-scatter.2 | all-reduce-scatter fusion | flops 712705 | bytes 2107904
  128.6 3.6 collective-permute-start.3
  137.3 4.5 concatenate.14
  141.8 2.2 fusion.49
  145.2 4.5 concatenate.13
  149.8 2.7 fusion.69
  159.6 3.4 fusion.75
  166.5 5.2 multiply_reduce_fusion
  181.4 3.5 fusion.18
  186.4 2.3 copy.94
  188.6 2.2 copy.93
  198.9 4.1 fusion.52
  203.1 11.8 %convolution_bitcast_fusion = f32[768,3,1536]{0,2,1:T(8,128)} fusion(bf16[3,454,1536]{2,1,0:T(8,128)(2,1)} %copy-done.48, bf16[1,454,768]{2,0,1:T(2,128)(2,1)} %all-gather), kind=kOutput, calls=%fused_computation.14 | convolution fusion | flops 3213361152 | bytes 19037184 | tf_op jit(solution)/shard_map/erf,rd->def/dot_general | solution.py:64
  214.9 20.7 %copy.100 = f32[768,3,1536]{2,1,0:T(4,128)} copy(f32[768,3,1536]{0,2,1:T(8,128)} %convolution_bitcast_fusion) | data formatting | bytes 28311552 | tf_op jit(solution)/shard_map/erf,rd->def/dot_general | solution.py:64
  237.2 86.0 %reduce-scatter.8.cloned.1.call-done = f32[48,2304]{1,0:T(8,128)} async-done(((f32[768,2304]{1,0:T(8,128)}), f32[48,2304]{1,0:T(8,128)}) %reduce-scatter.8.cloned.1.call-update) | async-done | bytes 442384 | tf_op jit(solution)/shard_map/reduce_scatter | solution.py:229
  325.3 11.7 %fusion.78 = f32[768,3,1536]{2,0,1:T(8,128)} fusion(bf16[454,768,1]{1,0,2:T(8,128)(2,1)} %reshape.272, bf16[3,454,1536]{2,1,0:T(8,128)(2,1)} %copy-done.47), kind=kOutput, calls=%fused_computation.127 | convolution fusion | flops 3213361152 | bytes 19037184 | tf_op jit(solution)/shard_map/rd,erf->def/dot_general | solution.py:67
  338.8 2.5 fusion.48
  342.4 35.8 %all-reduce.7 = (bf16[768]{0:T(1024)(128)(2,1)}, bf16[768]{0:T(1024)(128)(2,1)}) all-reduce(f32[768]{0:T(1024)} %get-tuple-element.42, f32[768]{0:T(1024)S(1)} %copy-done.37), channel_id=5, replica_groups=mesh['blk'=2,'dp'=16] {'dp'}, use_global_device_ids=true, to_apply=%region_17.18.clone | all-reduce | flops 1536 | bytes 9216
  380.2 5.6 all-reduce.8
  388.7 2.8 fusion.57
  391.5 265.0 %all-reduce.14.cloned.1.call-done = f32[768,3,1536]{2,1,0:T(4,128)} async-done(((f32[768,3,1536]{2,1,0:T(4,128)}), f32[768,3,1536]{2,1,0:T(4,128)}) %all-reduce.14.cloned.1.call-update) | async-done | bytes 14155792
  659.1 24.2 %all-reduce.16.cloned.1.call-done = (bf16[48,2304]{1,0:T(8,128)(2,1)}, bf16[48,768]{1,0:T(8,128)(2,1)}) async-done(((bf16[48,2304]{1,0:T(8,128)(2,1)}, bf16[48,768]{1,0:T(8,128)(2,1)}), (bf16[48,2304]{1,0:T(8,128)(2,1)}, bf16[48,768]{1,0:T(8,128)(2,1)})) %all-reduce.16.cloned.1.call-update) | async-done | bytes 294928 | tf_op jit(solution)/shard_map/psum | solution.py:235
  686.6 147.5 %reduce-scatter.12.cloned.1.call-done = f32[48,3,1536]{2,0,1:T(8,128)} async-done(((f32[768,3,1536]{2,0,1:T(8,128)}), f32[48,3,1536]{2,0,1:T(8,128)}) %reduce-scatter.12.cloned.1.call-update) | async-done | bytes 884752 | tf_op jit(solution)/shard_map/reduce_scatter | solution.py:147
  (183 shorter events, 85.2 us)
Async XLA Ops:
  7.2 3.1 copy-start
  7.2 228.5 %reduce-scatter.10.cloned.1.call-start = ((), (), s32[]{:S(2)}) async-start(), calls=%async_computation.4 | async-start | bytes 2506752 | tf_op jit(solution)/shard_map/reduce_scatter | solution.py:230
  8.5 3.9 copy-start.31
  12.4 10.6 %copy-start.44 = (s32[1,454]{1,0:T(1,128)S(1)}, s32[1,454]{1,0:T(1,128)}, u32[]{:S(2)}) copy-start(s32[1,454]{1,0:T(1,128)} %param.12) | copy-start | bytes 5452
  13.3 12.7 %copy-start.45 = (s32[1,454]{1,0:T(1,128)S(1)}, s32[1,454]{1,0:T(1,128)}, u32[]{:S(2)}) copy-start(s32[1,454]{1,0:T(1,128)} %param.11) | copy-start | bytes 5452
  13.3 39.6 %collective-permute-start = (bf16[227,1536]{1,0:T(8,128)(2,1)}, bf16[227,1536]{1,0:T(8,128)(2,1)}, u32[]{:S(2)}, u32[]{:S(2)}) collective-permute-start(bf16[227,1536]{1,0:T(8,128)(2,1)} %slice.31), channel_id=1, source_target_pairs={{0,16},{16,0},{1,17},{17,1},{2,18},{18,2},{3,19},{19,3},{4,20},{20... | collective-permute-start | bytes 2092040 | tf_op jit(solution)/shard_map/ppermute | solution.py:20
  85.4 8.1 copy-start.48
  85.4 8.1 copy-start.28
  85.4 8.1 copy-start.43
  85.4 17.9 %slice-start = ((s8[7077888]{0:T(1024)(128)(4,1)}), s8[4194304]{0:T(1024)(128)(4,1)S(1)}, s32[]{:S(2)}) async-start(s8[7077888]{0:T(1024)(128)(4,1)} %bitcast.183), calls=%async_computation.8 | async-start | bytes 8388608
  93.5 9.8 %slice-start.1 = ((s8[7077888]{0:T(1024)(128)(4,1)}), s8[2883584]{0:T(1024)(128)(4,1)S(1)}, s32[]{:S(2)}) async-start(s8[7077888]{0:T(1024)(128)(4,1)} %bitcast.183), calls=%async_computation.9 | async-start | bytes 5767168
  128.6 8.7 %collective-permute-start.3 = (bf16[5,768]{1,0:T(8,128)(2,1)}, bf16[5,768]{1,0:T(8,128)(2,1)}, u32[]{:S(2)}, u32[]{:S(2)}) collective-permute-start(bf16[5,768]{1,0:T(8,128)(2,1)} %slice.35), channel_id=1, source_target_pairs={{0,16},{1,17},{2,18},{3,19},{4,20},{5,21},{6,22},{7,23},{8,24},{9,... | collective-permute-start | bytes 23048
  135.4 9.8 %collective-permute-start.2 = (bf16[5,768]{1,0:T(8,128)(2,1)}, bf16[5,768]{1,0:T(8,128)(2,1)}, u32[]{:S(2)}, u32[]{:S(2)}) collective-permute-start(bf16[5,768]{1,0:T(8,128)(2,1)} %slice.34), channel_id=1, source_target_pairs={{0,16},{1,17},{2,18},{3,19},{4,20},{5,21},{6,22},{7,23},{8,24},{9,... | collective-permute-start | bytes 23048
  149.8 4.7 copy-start.19
  149.8 6.0 copy-start.25
  159.6 3.4 copy-start.4
  159.6 3.4 copy-start.14
  166.2 157.0 %reduce-scatter.8.cloned.1.call-start = ((), (), s32[]{:S(2)}) async-start(), calls=%async_computation.3 | async-start | bytes 7520256 | tf_op jit(solution)/shard_map/reduce_scatter | solution.py:229
  166.5 5.2 copy-start.2
  166.5 5.4 copy-start.5
  166.5 6.3 copy-start.6
  172.8 3.2 copy-start.15
  179.3 5.6 copy-start.10
  179.3 5.6 copy-start.16
  181.4 14.9 %collective-permute-start.1 = (bf16[227,1536]{1,0:T(8,128)(2,1)}, bf16[227,1536]{1,0:T(8,128)(2,1)}, u32[]{:S(2)}, u32[]{:S(2)}) collective-permute-start(bf16[227,1536]{1,0:T(8,128)(2,1)} %pad_maximum_fusion.1), channel_id=1, source_target_pairs={{0,16},{16,0},{1,17},{17,1},{2,18},{18,2},{3,19},{19,3},{4,20},{20... | collective-permute-start | bytes 2092040 | tf_op jit(solution)/shard_map/ppermute | solution.py:20
  192.9 6.0 copy-start.29
  192.9 6.0 copy-start.32
  192.9 6.0 copy-start.35
  203.1 453.4 %all-reduce.14.cloned.1.call-start = ((), (), s32[]{:S(2)}) async-start(), calls=%async_computation.6 | async-start | bytes 37748736
  235.6 447.7 %all-reduce.16.cloned.1.call-start = ((), (), s32[]{:S(2)}) async-start(), calls=%async_computation.7 | async-start | bytes 589824 | tf_op jit(solution)/shard_map/psum | solution.py:235
  324.9 509.2 %reduce-scatter.12.cloned.1.call-start = ((), (), s32[]{:S(2)}) async-start(), calls=%async_computation.5 | async-start | bytes 15040512 | tf_op jit(solution)/shard_map/reduce_scatter | solution.py:147
  338.8 3.6 copy-start.37
  (28 other events, 43.1 us)
Sparse Core Ops, SparseCore 0:
  166.3 63.1 reduce-scatter.9
  234.1 89.0 reduce-scatter.7
  327.0 329.3 all-reduce.13
  659.4 23.8 all-reduce.15
  688.4 145.6 reduce-scatter.11
where the time goes:
time: 843 us; the launch traced here: 841 us
  waiting for transfers between devices  523 us (62%)
  blocking collectives  94.2 us (11%)
  matrix products  88.3 us (10%)
  local copies, waits for them, and re-layouts  78.6 us (9%)
  other arithmetic  31.7 us (4%)
  between operations  15.6 us (2%)
  starting transfers between devices  9.11 us (1%)
    unnamed x8, waiting for transfers between devices  265 us
    reduce_scatter x1, waiting for transfers between devices, body(): lax.psum_scatter(grad_up_part, 'dp', scatter_dimension=0, tiled=True)  148 us
    reduce_scatter x1, waiting for transfers between devices, body(): lax.psum_scatter(grad_in_part, 'dp', scatter_dimension=0, tiled=True)  86 us
    unnamed x2, blocking collectives  55.5 us
    unnamed x113, local copies, waits for them, and re-layouts  30.8 us
    psum x1, waiting for transfers between devices, body(): lax.psum(summed_dp[1].astype(jnp.bfloat16), 'blk').astype(jnp.float32)  24.2 us
    all_gather x1, blocking collectives, body(): grad_gathered = lax.all_gather(grad_out, 'blk', axis=0, tiled=True)  22.7 us
    dot_general x1, local copies, waits for them, and re-layouts, expert_backward(): jnp.einsum('erf,rd->def', active, grad_rows, preferred_element_type=jnp.f...  20.7 us
  transfers between devices with their start and end apart: 9, of which 5 were waited for; matrix products, arithmetic and copies ran while one was open for 15% of the time, Pallas kernels for 0%

commit v1 on v0

v1 whole, which is shorter than its diff:
```python
import functools

import jax
import jax.numpy as jnp
import numpy as np
from jax import lax
from jax.experimental import pallas as pl
from jax.experimental.pallas import tpu as pltpu
from jax.sharding import PartitionSpec as P

HEADS = 12
HEAD_DIM = 64
EXPERTS = 3
EPSILON = 1e-05
NEGATIVE = -1e30
ROOT_HALF = 0.7071067811865476
INV_ROOT_TAU = 0.3989422804014327
SCALE = HEAD_DIM ** (-0.5)
LOG2_E = 1.4426950408889634
LANES = 128
INNER = 16
CORE, NEAR, MID, FAR = 1, 2, 4, 8

f32 = jnp.float32
bf16 = jnp.bfloat16

NN = ((1,), (0,))
NT = ((1,), (1,))
TN = ((0,), (0,))


def across_blk(value):
    return lax.ppermute(value, "blk", [(0, 1), (1, 0)])


def across_dp(value, bit):
    count = lax.axis_size("dp")
    return lax.ppermute(value, "dp", [(source, source ^ bit) for source in range(count)])


def after(value, *others):
    return lax.optimization_barrier((value, others))[0]


def dot(a, b, dims=NN):
    return lax.dot_general(a, b, (dims, ((), ())), preferred_element_type=f32)


def layer_norm_parts(values):
    row_mean = jnp.mean(values, axis=-1, keepdims=True)
    centred = values - row_mean
    row_var = jnp.mean(centred * centred, axis=-1, keepdims=True)
    scale = lax.rsqrt(row_var + EPSILON)
    return centred * scale, scale


def layer_norm_back(grad, gain, unit, scale):
    raised = grad * gain
    return scale * (
        raised
        - jnp.mean(raised, axis=-1, keepdims=True)
        - unit * jnp.mean(raised * unit, axis=-1, keepdims=True)
    )


def whole():
    return pl.BlockSpec(memory_space=pltpu.VMEM)


def scalars():
    return pl.BlockSpec(memory_space=pltpu.SMEM)


def shaped(shape, dtype):
    return jax.ShapeDtypeStruct(shape, dtype)


def held(shape, dtype):
    size = np.dtype(dtype).itemsize
    lead = int(np.prod(shape[:-2])) if len(shape) > 2 else 1
    deep = shape[-2] if len(shape) > 1 else 1
    return lead * -(-deep // 16) * 16 * -(-shape[-1] // LANES) * LANES * size


def call(kernel, name, out_shape, scratch=(), flops=0, small=0, room=4, aliases=None):
    def run(*operands):
        outs = out_shape if isinstance(out_shape, list) else [out_shape]
        moved = sum(held(a.shape, a.dtype) for a in operands[small:]) + sum(
            held(o.shape, o.dtype) for o in outs
        )
        need = moved + sum(held(v.shape, v.dtype) for v in scratch) + room * 2**20
        return pl.pallas_call(
            kernel,
            name=name,
            out_shape=out_shape,
            in_specs=[scalars()] * small + [whole()] * (len(operands) - small),
            out_specs=[whole()] * len(outs) if isinstance(out_shape, list) else whole(),
            scratch_shapes=list(scratch),
            input_output_aliases=aliases or {},
            compiler_params=pltpu.CompilerParams(vmem_limit_bytes=need),
            cost_estimate=pl.CostEstimate(flops=flops, bytes_accessed=moved, transcendentals=0),
        )(*operands)

    return run


def begin_kernel(
    count, deep, outer, place, side, ids, experts, own, gain, w_in,
    seg_col, seg_row, hot, hot_row, order, projected, normed_ref, token_rows,
):
    rows = seg_col.shape[0]
    span, width = rows // 2, own.shape[1]
    on_side = side[0] == 0

    def both(values):
        halves = values[0:1, :count], values[0:1, count:]
        pad = jnp.full((1, span - count), -1, jnp.int32)
        first = jnp.where(on_side, halves[0], halves[1])
        second = jnp.where(on_side, halves[1], halves[0])
        return jnp.broadcast_to(jnp.concatenate([first, pad, second, pad], axis=1), (8, rows))

    segments, expert = both(ids), both(experts)
    seg_row[...] = segments
    seg_col[...] = jnp.transpose(segments).astype(jnp.int32)
    kinds = lax.broadcasted_iota(jnp.int32, (8, rows), 0)
    hot_row[...] = (kinds == expert).astype(f32)
    turned = jnp.transpose(expert)
    hot[...] = (lax.broadcasted_iota(jnp.int32, (rows, 8), 1) == turned).astype(bf16)
    step = outer * deep
    lane = lax.broadcasted_iota(jnp.int32, (step, width), 1)
    low = lax.broadcasted_iota(jnp.int32, (step, width), 0)
    skip = low
    for late in range(1, outer):
        skip += jnp.where(low >= late * deep, (INNER - 1) * deep, 0)
    for block in range(INNER // 2):
        relative = ((block >> 2) & 1) * NEAR + ((block >> 1) & 1) * MID + (block & 1) * FAR
        base = (place[0] ^ relative) * deep
        order[block * step : (block + 1) * step, :] = (lane - base == skip).astype(f32).astype(bf16)
    token_rows[...] = jnp.zeros_like(token_rows)
    token_rows[0:count, :] = own[...].astype(f32)
    unit, _ = layer_norm_parts(token_rows[...])
    normed = (unit * gain[...]).astype(bf16)
    normed_ref[...] = normed
    projected[0:span, :] = dot(normed, w_in[...]).astype(bf16)


def begin(place, side, ids, experts, own, gain, w_in, deep, outer):
    count, width = own.shape
    span = -(-count // LANES) * LANES
    rows = 2 * span
    return call(
        functools.partial(begin_kernel, count, deep, outer),
        "begin",
        [
            shaped((rows, 8), jnp.int32),
            shaped((8, rows), jnp.int32),
            shaped((rows, 8), bf16),
            shaped((8, rows), f32),
            shaped((width // 2, width), bf16),
            shaped((rows, 3 * width), bf16),
            shaped((span, width), bf16),
            shaped((span, width), f32),
        ],
        flops=span * width * width * 6,
        small=2,
    )(place, side, ids, experts, own, gain, w_in)


def front_kernel(
    own_rows, own_normed, far, seg_col, seg_row, gain_one, gain_two, w_in, w_out, half_done,
    projected, packed, middle_ref, token_rows, lse_ref, bias,
):
    count, width = far.shape
    rows = projected.shape[0]
    span = rows // 2
    token_rows[0:span, :] = own_rows[...]
    token_rows[span:, :] = jnp.zeros((span, width), f32)
    token_rows[span : span + count, :] = far[...].astype(f32)
    unit, _ = layer_norm_parts(token_rows[span:, :])
    normed = (unit * gain_one[...]).astype(bf16)
    packed[1, :span, :] = own_normed[...]
    packed[1, span:, :] = normed
    projected[:span, :] = half_done[:span, :]
    projected[span:, :] = dot(normed, w_in[...]).astype(bf16)
    allowed = (seg_row[0:1, :] == 0) | (seg_row[0:1, :] == seg_col[:, 0:1])
    bias[...] = jnp.where(allowed, 0.0, NEGATIVE)
    lane = lax.broadcasted_iota(jnp.int32, (rows, LANES), 1)
    first = lane < HEAD_DIM
    lse_ref[...] = jnp.zeros_like(lse_ref)

    def pair(p, _):
        def columns(shift):
            return pl.ds(pl.multiple_of(shift + p * LANES, LANES), LANES)

        queries = projected[:, columns(0)] * jnp.asarray(SCALE, bf16)
        keys = projected[:, columns(width)]
        values = projected[:, columns(2 * width)]
        outs = []
        for head in range(2):
            mine = first if head == 0 else jnp.logical_not(first)
            scores = dot(jnp.where(mine, queries, jnp.zeros_like(queries)), keys, NT)
            scores = scores * LOG2_E + bias[...]
            peak = jnp.max(scores, axis=-1, keepdims=True)
            raised = jnp.exp2(scores - peak).astype(bf16)
            summed = dot(raised, jnp.where(mine, values, jnp.ones_like(values)))
            at = (1 - head) * HEAD_DIM
            total = summed[:, at : at + 1]
            outs.append(summed / total)
            lse_ref[...] = jnp.where(lane == 2 * p + head, peak + jnp.log2(total), lse_ref[...])
        packed[2, :, columns(0)] = jnp.where(first, outs[0], outs[1]).astype(bf16)
        return 0

    lax.fori_loop(0, width // LANES, pair, 0)
    middle = token_rows[...] + dot(packed[2], w_out[...])
    middle_ref[...] = middle
    unit, _ = layer_norm_parts(middle)
    packed[0] = (unit * gain_two[...]).astype(bf16)


def front(own_rows, own_normed, far, seg_col, seg_row, gain_one, gain_two, w_in, w_out, half_done):
    rows, three = half_done.shape
    width = three // 3
    return call(
        front_kernel,
        "front",
        [
            shaped((rows, three), bf16),
            shaped((3, rows, width), bf16),
            shaped((rows, width), f32),
            shaped((rows, width), f32),
            shaped((rows, LANES), f32),
        ],
        scratch=[pltpu.VMEM((rows, rows), f32)],
        flops=6_000_000_000,
        room=8,
    )(own_rows, own_normed, far, seg_col, seg_row, gain_one, gain_two, w_in, w_out, half_done)


def masked_rows(target, value, hot):
    span = value.shape[1]
    for e in range(EXPERTS):
        target[:, e * span : (e + 1) * span] = value * hot[:, e : e + 1]


def up_kernel(packed, hot, hot_row, own_grads, far_grads, weight, active_ref, slope_ref, message, masked):
    width, hidden = packed.shape[2], weight.shape[2]
    rows = packed.shape[1]
    masked_rows(masked, packed[0], hot)
    count, span = own_grads.shape[0], rows // 2
    message[...] = jnp.zeros_like(message)
    message[0:count, :] = own_grads[...]
    message[span : span + count, :] = far_grads[...]
    message[rows : rows + 8, :rows] = hot_row[...].astype(bf16)
    chunk = 512
    for n in range(0, hidden, chunk):
        upward = dot(
            masked[...], weight[:, :, n : n + chunk].reshape(EXPERTS * width, chunk)
        )
        half = 0.5 * (1.0 + lax.erf(upward * ROOT_HALF))
        active_ref[:, n : n + chunk] = (upward * half).astype(bf16)
        slope_ref[:, n : n + chunk] = half + upward * INV_ROOT_TAU * jnp.exp(-0.5 * upward * upward)


def up_forward(packed, hot, hot_row, own_grads, far_grads, up_weight):
    _, rows, width = packed.shape
    hidden = up_weight.shape[2]
    return call(
        up_kernel,
        "up_forward",
        [
            shaped((rows, hidden), bf16),
            shaped((rows, hidden), f32),
            shaped((rows + 16, width), bf16),
        ],
        scratch=[pltpu.VMEM((rows, EXPERTS * width), bf16)],
        flops=2 * rows * width * hidden * EXPERTS,
        room=6,
    )(packed, hot, hot_row, own_grads, far_grads, up_weight)


def grad_upward_kernel(message, hot, weight, slope, out_ref, masked):
    rows, hidden = out_ref.shape
    width = message.shape[1]
    masked_rows(masked, message[:rows, :], hot)
    chunk = 512
    for n in range(0, hidden, chunk):
        total = dot(masked[:, :width], weight[0, n : n + chunk, :], NT)
        for e in range(1, EXPERTS):
            total += dot(masked[:, e * width : (e + 1) * width], weight[e, n : n + chunk, :], NT)
        out_ref[:, n : n + chunk] = (total * slope[:, n : n + chunk]).astype(bf16)


def grad_upward_of(message, hot, down_weight, slope):
    rows, width = slope.shape[0], message.shape[1]
    hidden = down_weight.shape[1]
    return call(
        grad_upward_kernel,
        "grad_upward",
        shaped((rows, hidden), bf16),
        scratch=[pltpu.VMEM((rows, EXPERTS * width), bf16)],
        flops=2 * rows * width * hidden * EXPERTS,
        room=6,
    )(message, hot, down_weight, slope)


def hidden_back_kernel(dims, rows_ref, hot, weight, out_ref, masked):
    hidden, width = rows_ref.shape[1], out_ref.shape[1]
    masked_rows(masked, rows_ref[...], hot)
    chunk = 256
    for n in range(0, width, chunk):
        total = jnp.zeros((rows_ref.shape[0], chunk), f32)
        for e in range(EXPERTS):
            part = weight[e, n : n + chunk, :] if dims is NT else weight[e, :, n : n + chunk]
            total += dot(masked[:, e * hidden : (e + 1) * hidden], part, dims)
        out_ref[:, n : n + chunk] = total.astype(out_ref.dtype)


def hidden_back(dims, name, rows_ref, hot, weight):
    rows, hidden = rows_ref.shape
    width = weight.shape[1] if dims is NT else weight.shape[2]
    return call(
        functools.partial(hidden_back_kernel, dims),
        name,
        shaped((rows, width), bf16),
        scratch=[pltpu.VMEM((rows, EXPERTS * hidden), bf16)],
        flops=2 * rows * width * hidden * EXPERTS,
        room=6,
    )(rows_ref, hot, weight)


def picked_kernel(order, hot_own, hot_far, own, far, own_ref, far_ref):
    rows = own_ref.shape[2]
    for source, hot, target in ((own, hot_own, own_ref), (far, hot_far, far_ref)):
        values = source[0] if len(source.shape) == 3 else source[:rows, :]
        turned = dot(order[...], values, NT)
        for e in range(EXPERTS):
            target[e] = (turned * hot[e : e + 1, :rows].astype(f32)).astype(bf16)


def picked(order, hot_own, hot_far, own, far):
    rows = hot_own.shape[1]
    shape = shaped((EXPERTS, order.shape[0], rows), bf16)
    return call(
        picked_kernel,
        "picked",
        [shape, shape],
        flops=4 * order.shape[0] * order.shape[1] * rows,
    )(order, hot_own, hot_far, own, far)


def expert_grad_kernel(expert, a_own, a_far, b_own, b_far, keep_ref, send_ref):
    half = keep_ref.shape[0]
    chunk = 512
    for n in range(0, b_own.shape[1], chunk):
        both = dot(a_own[expert], b_own[:, n : n + chunk])
        both += dot(a_far[expert], b_far[:, n : n + chunk])
        keep_ref[:, n : n + chunk] = both[:half].astype(bf16)
        send_ref[:, n : n + chunk] = both[half:].astype(bf16)


def expert_grad(expert, a_own, a_far, b_own, b_far):
    _, wide, rows = a_own.shape
    hidden = b_own.shape[1]
    shape = shaped((wide // 2, hidden), bf16)
    return call(
        functools.partial(expert_grad_kernel, expert),
        "expert_grad",
        [shape, shape],
        flops=4 * wide * rows * hidden,
    )(a_own, a_far, b_own, b_far)


def attention_grad_kernel(order, own, far, g_own, g_far, keep_ref, send_ref):
    half = keep_ref.shape[0]
    rows, span = own.shape[1], g_own.shape[1]
    for plane, blocks in ((1, (0, 1, 2)), (2, (3,))):
        near = dot(order[...], own[plane], NT).astype(bf16)
        away = dot(order[...], far[plane], NT).astype(bf16)
        for at in blocks:
            both = dot(near, g_own[at * rows : (at + 1) * rows, :])
            both += dot(away, g_far[at * rows : (at + 1) * rows, :])
            keep_ref[:, at * span : (at + 1) * span] = both[:half].astype(bf16)
            send_ref[:, at * span : (at + 1) * span] = both[half:].astype(bf16)
    sums = g_own[4 * rows : 4 * rows + 16, :].astype(f32)
    sums += g_far[4 * rows : 4 * rows + 16, :].astype(f32)
    both = dot(order[:, :span], sums[0:8].astype(bf16), NT)
    both += dot(order[:, span:], sums[8:16].astype(bf16), NT)
    tail = jnp.concatenate([both, jnp.zeros((2 * half, LANES - 8), f32)], axis=1).astype(bf16)
    keep_ref[:, 4 * span :] = tail[:half]
    send_ref[:, 4 * span :] = tail[half:]


def attention_grad(order, own, far, g_own, g_far):
    shape = shaped((order.shape[0] // 2, 4 * g_own.shape[1] + LANES), bf16)
    return call(
        attention_grad_kernel,
        "attention_grad",
        [shape, shape],
        flops=2_500_000_000,
    )(order, own, far, g_own, g_far)


def back_kernel(
    side, part_own, part_far, grad_rows, middle, token_rows, gain_one, gain_two,
    w_out, w_in, projected, lse, seg_row, seg_col,
    message, gm_ref, gn_ref, gn_send, bias, branch_low, attended_back,
):
    rows, width = middle.shape
    span = rows // 2
    half = width // 2
    start = side[0] * half

    def mine_of(shift, extent=half):
        return pl.ds(pl.multiple_of(shift + start, LANES), extent)

    unit, scale = layer_norm_parts(middle[...])
    grad = part_own[...].astype(f32)
    grad += jnp.concatenate([part_far[span:, :], part_far[:span, :]], axis=0).astype(f32)
    gains_two = jnp.sum(grad * unit, axis=0, keepdims=True)
    grad_middle = grad_rows[:rows, :].astype(f32) + layer_norm_back(
        grad, gain_two[...], unit, scale
    )
    gm_ref[...] = grad_middle[:span]
    branch_low[...] = grad_middle.astype(bf16)
    attended_back[...] = dot(branch_low[...], w_out[mine_of(0), :], NT).astype(bf16)
    allowed = (seg_col[:, 0:1] == 0) | (seg_col[:, 0:1] == seg_row[0:1, :])
    bias[...] = jnp.where(allowed, 0.0, NEGATIVE)
    first = lax.broadcasted_iota(jnp.int32, (rows, LANES), 1) < HEAD_DIM
    on_side = side[0] == 0
    sums = jnp.transpose(lse[...])

    for p in range(half // LANES):
        def columns(shift):
            return pl.ds(pl.multiple_of(shift + start + p * LANES, LANES), LANES)

        queries = projected[:, columns(0)] * jnp.asarray(SCALE, bf16)
        keys, values = projected[:, columns(width)], projected[:, columns(2 * width)]
        grads = attended_back[:, p * LANES : (p + 1) * LANES]
        parts = []
        for head in range(2):
            mine = first if head == 0 else jnp.logical_not(first)
            zero = jnp.zeros_like(queries)
            at = 2 * p + head
            far_at = at + half // HEAD_DIM
            lse_row = jnp.where(on_side, sums[at : at + 1, :], sums[far_at : far_at + 1, :])
            scores = dot(keys, jnp.where(mine, queries, zero), NT) * LOG2_E + bias[...]
            probs = jnp.exp2(scores - lse_row)
            dprobs = dot(values, jnp.where(mine, grads, zero), NT)
            delta = jnp.sum(probs * dprobs, axis=0, keepdims=True)
            dscores = (probs * (dprobs - delta)).astype(bf16)
            parts.append(
                (
                    dot(dscores, keys, TN) * SCALE,
                    dot(dscores, queries),
                    dot(probs.astype(bf16), grads),
                )
            )
        for at in range(3):
            message[at * rows : (at + 1) * rows, p * LANES : (p + 1) * LANES] = jnp.where(
                first, parts[0][at], parts[1][at]
            ).astype(bf16)
    message[3 * rows : 4 * rows, :] = branch_low[:, mine_of(0)]
    grad_normed = dot(message[0:rows, :], w_in[:, mine_of(0)], NT)
    grad_normed += dot(message[rows : 2 * rows, :], w_in[:, mine_of(width)], NT)
    grad_normed += dot(message[2 * rows : 3 * rows, :], w_in[:, mine_of(2 * width)], NT)
    gn_ref[...] = grad_normed[:span]
    gn_send[...] = grad_normed[span:].astype(bf16)
    unit, _ = layer_norm_parts(token_rows[...])
    gains_one = jnp.sum(grad_normed * unit, axis=0, keepdims=True)
    blank = jnp.zeros((6, half), f32)
    message[4 * rows :, :] = jnp.concatenate(
        [
            gains_one[:, :half], gains_two[:, :half], blank,
            gains_one[:, half:], gains_two[:, half:], blank,
        ],
        axis=0,
    ).astype(bf16)


def back(
    side, part_own, part_far, grad_rows, middle, token_rows, gain_one, gain_two,
    w_out, w_in, projected, lse, seg_row, seg_col,
):
    rows, width = middle.shape
    half, span = width // 2, rows // 2
    return call(
        back_kernel,
        "back",
        [
            shaped((4 * rows + 16, half), bf16),
            shaped((span, width), f32),
            shaped((span, width), f32),
            shaped((span, width), bf16),
        ],
        scratch=[
            pltpu.VMEM((rows, rows), f32),
            pltpu.VMEM((rows, width), bf16),
            pltpu.VMEM((rows, half), bf16),
        ],
        flops=7_000_000_000,
        small=1,
        room=8,
    )(
        side, part_own, part_far, grad_rows, middle, token_rows, gain_one, gain_two,
        w_out, w_in, projected, lse, seg_row, seg_col,
    )


def last_kernel(gm, gn, gn_far, token_rows, gain, out_ref):
    count, span = out_ref.shape[0], gm.shape[0]
    unit, scale = layer_norm_parts(token_rows[...])
    grad = gn[...] + gn_far[...].astype(f32)
    total = gm[...] + layer_norm_back(grad, gain[...], unit, scale)
    out_ref[...] = total[:count].astype(bf16)


def last(gm, gn, gn_far, token_rows, gain, count):
    return call(last_kernel, "last", shaped((count, gm.shape[1]), bf16), flops=10_000_000)(
        gm, gn, gn_far, token_rows, gain
    )


def add_kernel(keep, far, keep_ref, send_ref):
    half = keep_ref.shape[0]
    total = keep[...].astype(f32) + far[...].astype(f32)
    keep_ref[...] = total[:half].astype(bf16)
    send_ref[...] = total[half:].astype(bf16)


def added(keep, far):
    count, wide = keep.shape
    shape = shaped((count // 2, wide), bf16)
    return call(add_kernel, "added", [shape, shape], flops=count * wide)(keep, far)


def finish_kernel(*refs):
    out_ref = refs[-1]
    for e in range(EXPERTS):
        out_ref[e] = refs[2 * e][...].astype(f32) + refs[2 * e + 1][...].astype(f32)


def finished(pairs):
    return call(
        finish_kernel,
        "finished",
        shaped((EXPERTS,) + pairs[0][0].shape, f32),
        flops=pairs[0][0].size * EXPERTS,
    )(*[part for pair in pairs for part in pair])


def body(
    tokens,
    segment_ids,
    expert_ids,
    norm_first,
    project_in,
    project_out,
    norm_second,
    up_weight,
    down_weight,
    cotangent,
):
    own_count, width = tokens.shape[1], tokens.shape[2]
    side = lax.axis_index("blk").astype(jnp.int32)[None]
    count = lax.axis_size("dp")
    place = (lax.axis_index("dp") % INNER).astype(jnp.int32)[None]
    outer = count // INNER
    deep = width // count
    half = width // 2
    gain_one, gain_two = norm_first[None], norm_second[None]

    own_tokens, own_grads = tokens[0], cotangent[0]
    far_tokens = across_blk(own_tokens)
    far_grads = across_blk(own_grads)
    seg_col, seg_row, hot, hot_row, order, half_done, own_normed, own_rows = begin(
        place, side, segment_ids, expert_ids, own_tokens, gain_one, project_in, deep, outer
    )
    rows = hot.shape[0]
    span = rows // 2
    projected, packed, middle, token_rows, lse = front(
        own_rows, own_normed, far_tokens, seg_col, seg_row, gain_one, gain_two,
        project_in, project_out, half_done,
    )
    active, slope, grad_rows = up_forward(packed, hot, hot_row, own_grads, far_grads, up_weight)
    active_far = across_dp(active, CORE)
    grad_rows_far = across_dp(grad_rows, CORE)
    hot_far = grad_rows_far[rows:]
    grad_upward = grad_upward_of(grad_rows, hot, down_weight, slope)
    grad_upward_far = across_dp(grad_upward, CORE)
    packed_far = across_dp(after(packed, grad_upward), CORE)

    cot_own, cot_far = picked(order, hot_row, hot_far, after(grad_rows, grad_upward), grad_rows_far)
    down_raw = [expert_grad(e, cot_own, cot_far, active, active_far) for e in range(EXPERTS)]
    part_own = hidden_back(NT, "grad_normed", after(grad_upward, down_raw), hot, up_weight)
    part_far = across_blk(part_own)
    two_own, two_far = picked(order, hot_row, hot_far, after(packed, part_own), packed_far)
    up_raw = [
        expert_grad(e, two_own, two_far, grad_upward, grad_upward_far) for e in range(EXPERTS)
    ]
    branch = hidden_back(NN, "branch", after(active, up_raw), hot, down_weight)
    branch_far = across_blk(branch[span:])
    layer_out = (
        middle[:own_count] + branch[:own_count].astype(f32) + branch_far[:own_count].astype(f32)
    ).astype(bf16)

    message, gm_own, gn_own, gn_send = back(
        side, after(part_own, branch), part_far, grad_rows, middle, token_rows,
        gain_one, gain_two, project_out, project_in, projected, lse, seg_row, seg_col,
    )
    message_far = across_dp(message, CORE)
    gn_far = across_blk(gn_send)
    in_raw = attention_grad(order, packed, packed_far, message, message_far)
    input_grad = last(gm_own, gn_own, gn_far, own_rows, gain_one, own_count)

    def reduced(keep, send):
        for bit in (NEAR, MID):
            keep, send = added(keep, across_dp(send, bit))
        return keep, across_dp(send, FAR)

    down_sum = finished([reduced(*raw) for raw in down_raw])
    up_sum = finished([reduced(*raw) for raw in up_raw])
    keep, far = reduced(*in_raw)
    in_sum = keep.astype(f32) + far.astype(f32)

    def over_outer(value, axis):
        if outer == 1:
            return value
        groups = [[o * INNER + i for o in range(outer)] for i in range(INNER)]
        return lax.psum_scatter(
            value, "dp", scatter_dimension=axis, tiled=True, axis_index_groups=groups
        )

    up_out = over_outer(up_sum, 1)
    down_out = over_outer(down_sum, 1).transpose(0, 2, 1)
    in_sum = over_outer(in_sum, 0)
    in_far = across_blk(in_sum.astype(bf16)).astype(f32)
    mine = in_sum[:, : 4 * half].reshape(deep, 4, half)
    theirs = in_far[:, : 4 * half].reshape(deep, 4, half)
    joined = jnp.where(
        side[0] == 0,
        jnp.stack([mine, theirs], axis=2),
        jnp.stack([theirs, mine], axis=2),
    ).reshape(deep, 4 * width)
    return (
        layer_out[None],
        input_grad[None],
        in_sum[:, 4 * half] + in_far[:, 4 * half],
        joined[:, : 3 * width],
        joined[:, 3 * width :],
        in_sum[:, 4 * half + 1],
        up_out,
        down_out,
    )


def solution(mesh):
    return jax.shard_map(
        body,
        mesh=mesh,
        in_specs=(
            P("dp", "blk", None),
            P("dp", None),
            P("dp", None),
            P(),
            P(),
            P(),
            P(),
            P(None, None, "blk"),
            P(None, "blk", None),
            P("dp", "blk", None),
        ),
        out_specs=(
            P("dp", "blk", None),
            P("dp", "blk", None),
            P("dp"),
            P("dp", None),
            P("dp", None),
            P("dp"),
            P(None, "dp", "blk"),
            P(None, "blk", "dp"),
        ),
        check_vma=False,
    )
```

time: 843 us -> 230 us (0.27)
  waiting for transfers between devices: 523 us -> 92 us
  blocking collectives: 94.2 us -> 0 us
  matrix products: 88.3 us -> 0 us
  Pallas kernels: 0 us -> 62 us
  local copies, waits for them, and re-layouts: 78.6 us -> 26.1 us
  starting transfers between devices: 9.11 us -> 40.1 us
  other arithmetic: 31.7 us -> 3.76 us
  between operations: 15.6 us -> 1.6 us
    unnamed x8 -> x0, waiting for transfers between devices: 265 us -> none
    reduce_scatter x3 -> x0, waiting for transfers between devices: 234 us -> none  [the longest x1 148 us: body(): lax.psum_scatter(grad_up_part, 'dp', scatter_dimension=0, tiled=True)]
    ppermute x2 -> x32, waiting for transfers between devices: 0.27 us -> 92 us  [the longest x26 81.1 us: across_dp(): lax.ppermute(value, 'dp', [(source, source ^ bit) for source in range(cou...]
    dot_general x24 -> x0, matrix products: 88.3 us -> none  [the longest x1 11.8 us: expert_backward(): jnp.einsum('erf,rd->def', active, grad_rows, preferred_element_type=jnp.f...]
    pallas_call x0 -> x33, Pallas kernels: none -> 62 us  [run(): pl.pallas_call(kernel, name=name, out_shape=out_shape, in_specs=[scalars(...]
    unnamed x2 -> x0, blocking collectives: 55.5 us -> none
    ppermute x2 -> x32, starting transfers between devices: 2.97 us -> 40.1 us  [the longest x26 31.5 us: across_dp(): lax.ppermute(value, 'dp', [(source, source ^ bit) for source in range(cou...]
    all_gather x2 -> x0, blocking collectives: 33.2 us -> none  [the longest x1 22.7 us: body(): grad_gathered = lax.all_gather(grad_out, 'blk', axis=0, tiled=True)]
  transfers between devices with their start and end apart: 9 -> 32, of which waited for: 5 -> 14; matrix products, arithmetic and copies ran while one was open for 15% -> 2% of each run, Pallas kernels for 0% -> 19%
where the time goes in v1:
time: 230 us; the launch traced here: 226 us
  waiting for transfers between devices  92 us (40%)
  Pallas kernels  62 us (27%)
  starting transfers between devices  40.1 us (17%)
  local copies, waits for them, and re-layouts  26.1 us (11%)
  other arithmetic  3.76 us (2%)
    ppermute x26, waiting for transfers between devices, across_dp(): lax.ppermute(value, 'dp', [(source, source ^ bit) for source in range(cou...  81.1 us
    pallas_call x33, Pallas kernels, run(): pl.pallas_call(kernel, name=name, out_shape=out_shape, in_specs=[scalars(...  62 us
    ppermute x26, starting transfers between devices, across_dp(): lax.ppermute(value, 'dp', [(source, source ^ bit) for source in range(cou...  31.5 us
    unnamed x78, local copies, waits for them, and re-layouts  22.1 us
    ppermute x6, waiting for transfers between devices, across_blk(): return lax.ppermute(value, 'blk', [(0, 1), (1, 0)])  10.9 us
    ppermute x6, starting transfers between devices, across_blk(): return lax.ppermute(value, 'blk', [(0, 1), (1, 0)])  8.63 us
  transfers between devices with their start and end apart: 32, of which 14 were waited for; matrix products, arithmetic and copies ran while one was open for 2% of the time, Pallas kernels for 19%

profile of v1, /device:TPU:0, one launch (start us, length us, event | category | flops | bytes accessed | tf_op | source)
XLA Modules:
  0.0 225.7 jit_solution(2565035042910096108)
XLA Ops:
  0.6 3.0 %collective-permute-start = (bf16[227,768]{1,0:T(8,128)(2,1)}, bf16[227,768]{1,0:T(8,128)(2,1)S(1)}, u32[]{:S(2)}, u32[]{:S(2)}) collective-permute-start(bf16[227,768]{1,0:T(8,128)(2,1)} %bitcast.8), channel_id=1, source_target_pairs={{0,16},{16,0},{1,17},{17,1},{2,18},{18,2},{3,19},{19,3},{4,20},{20... | collective-permute-start | bytes 1046024 | tf_op jit(solution)/shard_map/ppermute | solution.py:33
  5.1 2.0 copy-done
  10.9 2.1 collective-permute-done.far
  14.3 10.1 %front.1 = (bf16[512,2304]{1,0:T(8,128)(2,1)S(1)}, bf16[3,512,768]{2,1,0:T(8,128)(2,1)S(1)}, f32[512,768]{1,0:T(8,128)S(1)}, f32[512,768]{1,0:T(8,128)S(1)}, f32[512,128]{1,0:T(8,128)S(1)}) custom-call(f32[256,768]{1,0:T(8,128)S(1)} %get-tuple-element.80.own_rows.token_rows, bf16[256,768]{1,0:T(8,128)(2,1)S(1)} %get-tuple-element.81.own_normed, ...), custom_call_target="tpu_custom_call" | custom-call | flops 6000000000 | bytes 17145856 | tf_op jit(solution)/shard_map/front/pallas_call | solution.py:92
  24.5 4.5 %copy-done.26 = bf16[3,768,1536]{2,1,0:T(8,128)(2,1)S(1)} copy-done((bf16[3,768,1536]{2,1,0:T(8,128)(2,1)S(1)}, bf16[3,768,1536]{2,1,0:T(8,128)(2,1)}, u32[]{:S(2)}) %copy-start.26) | copy-done | bytes 7077912
  29.0 4.7 %up_forward.1 = (bf16[512,1536]{1,0:T(8,128)(2,1)S(1)}, f32[512,1536]{1,0:T(8,128)S(1)}, bf16[528,768]{1,0:T(8,128)(2,1)S(1)}) custom-call(bf16[3,512,768]{2,1,0:T(8,128)(2,1)S(1)} %get-tuple-element.104.packed.own, bf16[512,8]{1,0:T(8,128)(2,1)S(1)} %get-tuple-element.87.hot, f32[8,512]{1,0:T(8,128)S(1)} %get-tuple-element.88.hot_row.hot_own, ...), custom_call_target="tpu_custom_call" | custom-call | flops 3623878656 | bytes 15867904 | tf_op jit(solution)/shard_map/up_forward/pallas_call | solution.py:92
  33.8 3.0 %copy-done.27 = bf16[3,1536,768]{2,1,0:T(8,128)(2,1)S(1)} copy-done((bf16[3,1536,768]{2,1,0:T(8,128)(2,1)S(1)}, bf16[3,1536,768]{2,1,0:T(8,128)(2,1)}, u32[]{:S(2)}) %copy-start.27) | copy-done | bytes 7077912
  36.8 3.9 %grad_upward.1.rows_ref.b_own = bf16[512,1536]{1,0:T(8,128)(2,1)S(1)} custom-call(bf16[528,768]{1,0:T(8,128)(2,1)S(1)} %get-tuple-element.93.message.own.grad_rows, bf16[512,8]{1,0:T(8,128)(2,1)S(1)} %get-tuple-element.87.hot, bf16[3,1536,768]{2,1,0:T(8,128)(2,1)S(1)} %copy-done.27, f32[512,1536]{1,0:T(8,128)S(1)} %get-tuple-element.92.slope), custom_call_target="tpu_custom_call" | custom-call | flops 3623878656 | bytes 12738560 | tf_op jit(solution)/shard_map/grad_upward/pallas_call | solution.py:92
  41.8 6.9 %collective-permute-done.2.far = bf16[528,768]{1,0:T(8,128)(2,1)S(1)} collective-permute-done((bf16[528,768]{1,0:T(8,128)(2,1)S(1)}, bf16[528,768]{1,0:T(8,128)(2,1)S(1)}, u32[]{:S(2)}, u32[]{:S(2)}) %collective-permute-start.2) | collective-permute-done | bytes 811040 | tf_op jit(solution)/shard_map/ppermute | solution.py:38
  53.8 4.1 %grad_normed.1.part_own = bf16[512,768]{1,0:T(8,128)(2,1)S(1)} custom-call(bf16[512,1536]{1,0:T(8,128)(2,1)S(1)} %grad_upward.1.rows_ref.b_own, bf16[512,8]{1,0:T(8,128)(2,1)S(1)} %get-tuple-element.87.hot, bf16[3,768,1536]{2,1,0:T(8,128)(2,1)S(1)} %bitcast.11), custom_call_target="tpu_custom_call" | custom-call | flops 3623878656 | bytes 9568256 | tf_op jit(solution)/shard_map/grad_normed/pallas_call | solution.py:92
  57.9 2.1 collective-permute-start.7
  65.2 3.9 %branch.1 = bf16[512,768]{1,0:T(8,128)(2,1)S(1)} custom-call(bf16[512,1536]{1,0:T(8,128)(2,1)S(1)} %get-tuple-element.113.b_own.rows_ref, bf16[512,8]{1,0:T(8,128)(2,1)S(1)} %get-tuple-element.87.hot, bf16[3,1536,768]{2,1,0:T(8,128)(2,1)S(1)} %bitcast.13), custom_call_target="tpu_custom_call" | custom-call | flops 3623878656 | bytes 9568256 | tf_op jit(solution)/shard_map/branch/pallas_call | solution.py:92
  69.1 8.8 %collective-permute-done.7.part_far = bf16[512,768]{1,0:T(8,128)(2,1)S(1)} collective-permute-done((bf16[512,768]{1,0:T(8,128)(2,1)S(1)}, bf16[512,768]{1,0:T(8,128)(2,1)S(1)}, u32[]{:S(2)}, u32[]{:S(2)}) %collective-permute-start.7) | collective-permute-done | bytes 786464 | tf_op jit(solution)/shard_map/ppermute | solution.py:33
  77.9 10.3 %back.1 = (bf16[2064,384]{1,0:T(8,128)(2,1)S(1)}, f32[256,768]{1,0:T(8,128)S(1)}, f32[256,768]{1,0:T(8,128)S(1)}, bf16[256,768]{1,0:T(8,128)(2,1)}) custom-call(s32[1]{0:T(128)} %bitcast.1.side, bf16[512,768]{1,0:T(8,128)(2,1)S(1)} %grad_normed.1.part_own, bf16[512,768]{1,0:T(8,128)(2,1)S(1)} %collective-permute-done.7.part_far, ...), custom_call_target="tpu_custom_call" | custom-call | flops 7000000000 | bytes 16814080 | tf_op jit(solution)/shard_map/back/pallas_call | solution.py:92
  92.0 3.3 %attention_grad.1 = (bf16[192,1664]{1,0:T(8,128)(2,1)S(1)}, bf16[192,1664]{1,0:T(8,128)(2,1)S(1)}) custom-call(bf16[384,768]{1,0:T(8,128)(2,1)S(1)} %get-tuple-element.90.order, bf16[3,512,768]{2,1,0:T(8,128)(2,1)S(1)} %get-tuple-element.104.packed.own, bf16[3,512,768]{2,1,0:T(8,128)(2,1)S(1)} %collective-permute-done.4.far, ...), custom_call_target="tpu_custom_call" | custom-call | flops 2500000000 | bytes 9756672 | tf_op jit(solution)/shard_map/attention_grad/pallas_call | solution.py:92
  96.8 7.6 %collective-permute-done.29.far = bf16[192,1536]{1,0:T(8,128)(2,1)S(1)} collective-permute-done((bf16[192,1536]{1,0:T(8,128)(2,1)S(1)}, bf16[192,1536]{1,0:T(8,128)(2,1)S(1)}, u32[]{:S(2)}, u32[]{:S(2)}) %collective-permute-start.29) | collective-permute-done | bytes 589856 | tf_op jit(solution)/shard_map/ppermute | solution.py:38
  106.4 10.6 %collective-permute-done.26.far = bf16[192,1536]{1,0:T(8,128)(2,1)S(1)} collective-permute-done((bf16[192,1536]{1,0:T(8,128)(2,1)S(1)}, bf16[192,1536]{1,0:T(8,128)(2,1)S(1)}, u32[]{:S(2)}, u32[]{:S(2)}) %collective-permute-start.26) | collective-permute-done | bytes 589856 | tf_op jit(solution)/shard_map/ppermute | solution.py:38
  117.1 1.9 collective-permute-start.27
  119.0 10.6 %collective-permute-done.23.far = bf16[192,1536]{1,0:T(8,128)(2,1)S(1)} collective-permute-done((bf16[192,1536]{1,0:T(8,128)(2,1)S(1)}, bf16[192,1536]{1,0:T(8,128)(2,1)S(1)}, u32[]{:S(2)}, u32[]{:S(2)}) %collective-permute-start.23) | collective-permute-done | bytes 589856 | tf_op jit(solution)/shard_map/ppermute | solution.py:38
  129.8 1.9 collective-permute-start.24
  135.3 8.1 %collective-permute-done.10.far = bf16[192,1664]{1,0:T(8,128)(2,1)S(1)} collective-permute-done((bf16[192,1664]{1,0:T(8,128)(2,1)S(1)}, bf16[192,1664]{1,0:T(8,128)(2,1)S(1)}, u32[]{:S(2)}, u32[]{:S(2)}) %collective-permute-start.10) | collective-permute-done | bytes 639008 | tf_op jit(solution)/shard_map/ppermute | solution.py:38
  143.3 2.8 %collective-permute-start.31 = (bf16[48,1536]{1,0:T(8,128)(2,1)S(1)}, bf16[48,1536]{1,0:T(8,128)(2,1)S(1)}, u32[]{:S(2)}, u32[]{:S(2)}) collective-permute-start(bf16[48,1536]{1,0:T(8,128)(2,1)S(1)} %get-tuple-element.151), channel_id=1, source_target_pairs={{0,8},{1,9},{2,10},{3,11},{4,12},{5,13},{6,14},{7,15},{8,0},{9,1},... | collective-permute-start | bytes 442376 | tf_op jit(solution)/shard_map/ppermute | solution.py:38
  148.0 4.7 %collective-permute-done.31.refs_5_ = bf16[48,1536]{1,0:T(8,128)(2,1)S(1)} collective-permute-done((bf16[48,1536]{1,0:T(8,128)(2,1)S(1)}, bf16[48,1536]{1,0:T(8,128)(2,1)S(1)}, u32[]{:S(2)}, u32[]{:S(2)}) %collective-permute-start.31) | collective-permute-done | bytes 147488 | tf_op jit(solution)/shard_map/ppermute | solution.py:38
  153.8 8.0 %collective-permute-done.28.refs_3_ = bf16[48,1536]{1,0:T(8,128)(2,1)S(1)} collective-permute-done((bf16[48,1536]{1,0:T(8,128)(2,1)S(1)}, bf16[48,1536]{1,0:T(8,128)(2,1)S(1)}, u32[]{:S(2)}, u32[]{:S(2)}) %collective-permute-start.28) | collective-permute-done | bytes 147488 | tf_op jit(solution)/shard_map/ppermute | solution.py:38
  166.1 2.6 %collective-permute-done.17.far = bf16[192,1536]{1,0:T(8,128)(2,1)S(1)} collective-permute-done((bf16[192,1536]{1,0:T(8,128)(2,1)S(1)}, bf16[192,1536]{1,0:T(8,128)(2,1)S(1)}, u32[]{:S(2)}, u32[]{:S(2)}) %collective-permute-start.17) | collective-permute-done | bytes 589856 | tf_op jit(solution)/shard_map/ppermute | solution.py:38
  171.9 9.0 %collective-permute-done.14.far = bf16[192,1536]{1,0:T(8,128)(2,1)S(1)} collective-permute-done((bf16[192,1536]{1,0:T(8,128)(2,1)S(1)}, bf16[192,1536]{1,0:T(8,128)(2,1)S(1)}, u32[]{:S(2)}, u32[]{:S(2)}) %collective-permute-start.14) | collective-permute-done | bytes 589856 | tf_op jit(solution)/shard_map/ppermute | solution.py:38
  185.8 2.8 %collective-permute-start.12 = (bf16[48,1664]{1,0:T(8,128)(2,1)}, bf16[48,1664]{1,0:T(8,128)(2,1)}, u32[]{:S(2)}, u32[]{:S(2)}) collective-permute-start(bf16[48,1664]{1,0:T(8,128)(2,1)} %get-tuple-element.127), channel_id=1, source_target_pairs={{0,8},{1,9},{2,10},{3,11},{4,12},{5,13},{6,14},{7,15},{8,0},{9,1},... | collective-permute-start | bytes 479240 | tf_op jit(solution)/shard_map/ppermute | solution.py:38
  200.4 2.6 %collective-permute-start.19 = (bf16[48,1536]{1,0:T(8,128)(2,1)S(1)}, bf16[48,1536]{1,0:T(8,128)(2,1)S(1)}, u32[]{:S(2)}, u32[]{:S(2)}) collective-permute-start(bf16[48,1536]{1,0:T(8,128)(2,1)S(1)} %get-tuple-element.135), channel_id=1, source_target_pairs={{0,8},{1,9},{2,10},{3,11},{4,12},{5,13},{6,14},{7,15},{8,0},{9,1},... | collective-permute-start | bytes 442376 | tf_op jit(solution)/shard_map/ppermute | solution.py:38
  205.8 1.9 fusion
  207.8 7.0 %collective-permute-done.22.refs_5_ = bf16[48,1536]{1,0:T(8,128)(2,1)S(1)} collective-permute-done((bf16[48,1536]{1,0:T(8,128)(2,1)S(1)}, bf16[48,1536]{1,0:T(8,128)(2,1)S(1)}, u32[]{:S(2)}, u32[]{:S(2)}) %collective-permute-start.22) | collective-permute-done | bytes 147488 | tf_op jit(solution)/shard_map/ppermute | solution.py:38
  214.8 3.2 %collective-permute-done.19.refs_3_ = bf16[48,1536]{1,0:T(8,128)(2,1)S(1)} collective-permute-done((bf16[48,1536]{1,0:T(8,128)(2,1)S(1)}, bf16[48,1536]{1,0:T(8,128)(2,1)S(1)}, u32[]{:S(2)}, u32[]{:S(2)}) %collective-permute-start.19) | collective-permute-done | bytes 147488 | tf_op jit(solution)/shard_map/ppermute | solution.py:38
  218.0 2.7 %collective-permute-done.16.refs_1_ = bf16[48,1536]{1,0:T(8,128)(2,1)S(1)} collective-permute-done((bf16[48,1536]{1,0:T(8,128)(2,1)S(1)}, bf16[48,1536]{1,0:T(8,128)(2,1)S(1)}, u32[]{:S(2)}, u32[]{:S(2)}) %collective-permute-start.16) | collective-permute-done | bytes 147488 | tf_op jit(solution)/shard_map/ppermute | solution.py:38
  (162 shorter events, 63.1 us)
Async XLA Ops:
  0.6 12.4 %collective-permute-start = (bf16[227,768]{1,0:T(8,128)(2,1)}, bf16[227,768]{1,0:T(8,128)(2,1)S(1)}, u32[]{:S(2)}, u32[]{:S(2)}) collective-permute-start(bf16[227,768]{1,0:T(8,128)(2,1)} %bitcast.8), channel_id=1, source_target_pairs={{0,16},{16,0},{1,17},{17,1},{2,18},{18,2},{3,19},{19,3},{4,20},{20... | collective-permute-start | bytes 1046024 | tf_op jit(solution)/shard_map/ppermute | solution.py:33
  3.7 20.8 %collective-permute-start.1 = (bf16[227,768]{1,0:T(8,128)(2,1)}, bf16[227,768]{1,0:T(8,128)(2,1)S(1)}, u32[]{:S(2)}, u32[]{:S(2)}) collective-permute-start(bf16[227,768]{1,0:T(8,128)(2,1)} %bitcast.14), channel_id=1, source_target_pairs={{0,16},{16,0},{1,17},{17,1},{2,18},{18,2},{3,19},{19,3},{4,20},{20... | collective-permute-start | bytes 1046024 | tf_op jit(solution)/shard_map/ppermute | solution.py:33
  40.7 19.4 %collective-permute-start.4 = (bf16[3,512,768]{2,1,0:T(8,128)(2,1)S(1)}, bf16[3,512,768]{2,1,0:T(8,128)(2,1)S(1)}, u32[]{:S(2)}, u32[]{:S(2)}) collective-permute-start(bf16[3,512,768]{2,1,0:T(8,128)(2,1)S(1)} %get-tuple-element.104.packed.own), channel_id=1, source_target_pairs={{0,1},{1,0},{2,3},{3,2},{4,5},{5,4},{6,7},{7,6},{8,9},{9,8},{10,11... | collective-permute-start | bytes 7077896 | tf_op jit(solution)/shard_map/ppermute | solution.py:38
  40.8 8.8 %collective-permute-start.3 = (bf16[512,1536]{1,0:T(8,128)(2,1)S(1)}, bf16[512,1536]{1,0:T(8,128)(2,1)S(1)}, u32[]{:S(2)}, u32[]{:S(2)}) collective-permute-start(bf16[512,1536]{1,0:T(8,128)(2,1)S(1)} %get-tuple-element.113.b_own.rows_ref), channel_id=1, source_target_pairs={{0,1},{1,0},{2,3},{3,2},{4,5},{5,4},{6,7},{7,6},{8,9},{9,8},{10,11... | collective-permute-start | bytes 4718600 | tf_op jit(solution)/shard_map/ppermute | solution.py:38
  41.3 7.4 %collective-permute-start.2 = (bf16[528,768]{1,0:T(8,128)(2,1)S(1)}, bf16[528,768]{1,0:T(8,128)(2,1)S(1)}, u32[]{:S(2)}, u32[]{:S(2)}) collective-permute-start(bf16[528,768]{1,0:T(8,128)(2,1)S(1)} %get-tuple-element.93.message.own.grad_rows), channel_id=1, source_target_pairs={{0,1},{1,0},{2,3},{3,2},{4,5},{5,4},{6,7},{7,6},{8,9},{9,8},{10,11... | collective-permute-start | bytes 2433032 | tf_op jit(solution)/shard_map/ppermute | solution.py:38
  41.4 19.6 %collective-permute-start.5 = (bf16[512,1536]{1,0:T(8,128)(2,1)S(1)}, bf16[512,1536]{1,0:T(8,128)(2,1)S(1)}, u32[]{:S(2)}, u32[]{:S(2)}) collective-permute-start(bf16[512,1536]{1,0:T(8,128)(2,1)S(1)} %grad_upward.1.rows_ref.b_own), channel_id=1, source_target_pairs={{0,1},{1,0},{2,3},{3,2},{4,5},{5,4},{6,7},{7,6},{8,9},{9,8},{10,11... | collective-permute-start | bytes 4718600 | tf_op jit(solution)/shard_map/ppermute | solution.py:38
  57.9 20.0 %collective-permute-start.7 = (bf16[512,768]{1,0:T(8,128)(2,1)S(1)}, bf16[512,768]{1,0:T(8,128)(2,1)S(1)}, u32[]{:S(2)}, u32[]{:S(2)}) collective-permute-start(bf16[512,768]{1,0:T(8,128)(2,1)S(1)} %grad_normed.1.part_own), channel_id=1, source_target_pairs={{0,16},{16,0},{1,17},{17,1},{2,18},{18,2},{3,19},{19,3},{4,20},{20... | collective-permute-start | bytes 2359304 | tf_op jit(solution)/shard_map/ppermute | solution.py:33
  88.2 3.8 %collective-permute-start.9 = (bf16[2064,384]{1,0:T(8,128)(2,1)S(1)}, bf16[2064,384]{1,0:T(8,128)(2,1)S(1)}, u32[]{:S(2)}, u32[]{:S(2)}) collective-permute-start(bf16[2064,384]{1,0:T(8,128)(2,1)S(1)} %get-tuple-element.121.g_own), channel_id=1, source_target_pairs={{0,1},{1,0},{2,3},{3,2},{4,5},{5,4},{6,7},{7,6},{8,9},{9,8},{10,11... | collective-permute-start | bytes 4755464 | tf_op jit(solution)/shard_map/ppermute | solution.py:38
  88.2 16.1 %collective-permute-start.29 = (bf16[192,1536]{1,0:T(8,128)(2,1)S(1)}, bf16[192,1536]{1,0:T(8,128)(2,1)S(1)}, u32[]{:S(2)}, u32[]{:S(2)}) collective-permute-start(bf16[192,1536]{1,0:T(8,128)(2,1)S(1)} %get-tuple-element.101), channel_id=1, source_target_pairs={{0,2},{1,3},{2,0},{3,1},{4,6},{5,7},{6,4},{7,5},{8,10},{9,11},{10,... | collective-permute-start | bytes 1769480 | tf_op jit(solution)/shard_map/ppermute | solution.py:38
  90.0 27.0 %collective-permute-start.26 = (bf16[192,1536]{1,0:T(8,128)(2,1)S(1)}, bf16[192,1536]{1,0:T(8,128)(2,1)S(1)}, u32[]{:S(2)}, u32[]{:S(2)}) collective-permute-start(bf16[192,1536]{1,0:T(8,128)(2,1)S(1)} %get-tuple-element.99), channel_id=1, source_target_pairs={{0,2},{1,3},{2,0},{3,1},{4,6},{5,7},{6,4},{7,5},{8,10},{9,11},{10,... | collective-permute-start | bytes 1769480 | tf_op jit(solution)/shard_map/ppermute | solution.py:38
  90.3 39.4 %collective-permute-start.23 = (bf16[192,1536]{1,0:T(8,128)(2,1)S(1)}, bf16[192,1536]{1,0:T(8,128)(2,1)S(1)}, u32[]{:S(2)}, u32[]{:S(2)}) collective-permute-start(bf16[192,1536]{1,0:T(8,128)(2,1)S(1)} %get-tuple-element.97), channel_id=1, source_target_pairs={{0,2},{1,3},{2,0},{3,1},{4,6},{5,7},{6,4},{7,5},{8,10},{9,11},{10,... | collective-permute-start | bytes 1769480 | tf_op jit(solution)/shard_map/ppermute | solution.py:38
  95.3 48.0 %collective-permute-start.10 = (bf16[192,1664]{1,0:T(8,128)(2,1)S(1)}, bf16[192,1664]{1,0:T(8,128)(2,1)S(1)}, u32[]{:S(2)}, u32[]{:S(2)}) collective-permute-start(bf16[192,1664]{1,0:T(8,128)(2,1)S(1)} %get-tuple-element.123), channel_id=1, source_target_pairs={{0,2},{1,3},{2,0},{3,1},{4,6},{5,7},{6,4},{7,5},{8,10},{9,11},{10,... | collective-permute-start | bytes 1916936 | tf_op jit(solution)/shard_map/ppermute | solution.py:38
  104.5 28.6 %collective-permute-start.30 = (bf16[96,1536]{1,0:T(8,128)(2,1)S(1)}, bf16[96,1536]{1,0:T(8,128)(2,1)S(1)}, u32[]{:S(2)}, u32[]{:S(2)}) collective-permute-start(bf16[96,1536]{1,0:T(8,128)(2,1)S(1)} %get-tuple-element.149), channel_id=1, source_target_pairs={{0,4},{1,5},{2,6},{3,7},{4,0},{5,1},{6,2},{7,3},{8,12},{9,13},{10,... | collective-permute-start | bytes 884744 | tf_op jit(solution)/shard_map/ppermute | solution.py:38
  117.1 16.5 %collective-permute-start.27 = (bf16[96,1536]{1,0:T(8,128)(2,1)S(1)}, bf16[96,1536]{1,0:T(8,128)(2,1)S(1)}, u32[]{:S(2)}, u32[]{:S(2)}) collective-permute-start(bf16[96,1536]{1,0:T(8,128)(2,1)S(1)} %get-tuple-element.145), channel_id=1, source_target_pairs={{0,4},{1,5},{2,6},{3,7},{4,0},{5,1},{6,2},{7,3},{8,12},{9,13},{10,... | collective-permute-start | bytes 884744 | tf_op jit(solution)/shard_map/ppermute | solution.py:38
  129.8 16.5 %collective-permute-start.24 = (bf16[96,1536]{1,0:T(8,128)(2,1)S(1)}, bf16[96,1536]{1,0:T(8,128)(2,1)S(1)}, u32[]{:S(2)}, u32[]{:S(2)}) collective-permute-start(bf16[96,1536]{1,0:T(8,128)(2,1)S(1)} %get-tuple-element.141), channel_id=1, source_target_pairs={{0,4},{1,5},{2,6},{3,7},{4,0},{5,1},{6,2},{7,3},{8,12},{9,13},{10,... | collective-permute-start | bytes 884744 | tf_op jit(solution)/shard_map/ppermute | solution.py:38
  131.6 32.5 %collective-permute-start.20 = (bf16[192,1536]{1,0:T(8,128)(2,1)S(1)}, bf16[192,1536]{1,0:T(8,128)(2,1)S(1)}, u32[]{:S(2)}, u32[]{:S(2)}) collective-permute-start(bf16[192,1536]{1,0:T(8,128)(2,1)S(1)} %get-tuple-element.112), channel_id=1, source_target_pairs={{0,2},{1,3},{2,0},{3,1},{4,6},{5,7},{6,4},{7,5},{8,10},{9,11},{10,... | collective-permute-start | bytes 1769480 | tf_op jit(solution)/shard_map/ppermute | solution.py:38
  133.1 35.5 %collective-permute-start.17 = (bf16[192,1536]{1,0:T(8,128)(2,1)S(1)}, bf16[192,1536]{1,0:T(8,128)(2,1)S(1)}, u32[]{:S(2)}, u32[]{:S(2)}) collective-permute-start(bf16[192,1536]{1,0:T(8,128)(2,1)S(1)} %get-tuple-element.110), channel_id=1, source_target_pairs={{0,2},{1,3},{2,0},{3,1},{4,6},{5,7},{6,4},{7,5},{8,10},{9,11},{10,... | collective-permute-start | bytes 1769480 | tf_op jit(solution)/shard_map/ppermute | solution.py:38
  133.7 47.2 %collective-permute-start.14 = (bf16[192,1536]{1,0:T(8,128)(2,1)S(1)}, bf16[192,1536]{1,0:T(8,128)(2,1)S(1)}, u32[]{:S(2)}, u32[]{:S(2)}) collective-permute-start(bf16[192,1536]{1,0:T(8,128)(2,1)S(1)} %get-tuple-element.108), channel_id=1, source_target_pairs={{0,2},{1,3},{2,0},{3,1},{4,6},{5,7},{6,4},{7,5},{8,10},{9,11},{10,... | collective-permute-start | bytes 1769480 | tf_op jit(solution)/shard_map/ppermute | solution.py:38
  143.3 9.4 %collective-permute-start.31 = (bf16[48,1536]{1,0:T(8,128)(2,1)S(1)}, bf16[48,1536]{1,0:T(8,128)(2,1)S(1)}, u32[]{:S(2)}, u32[]{:S(2)}) collective-permute-start(bf16[48,1536]{1,0:T(8,128)(2,1)S(1)} %get-tuple-element.151), channel_id=1, source_target_pairs={{0,8},{1,9},{2,10},{3,11},{4,12},{5,13},{6,14},{7,15},{8,0},{9,1},... | collective-permute-start | bytes 442376 | tf_op jit(solution)/shard_map/ppermute | solution.py:38
  146.3 37.2 %collective-permute-start.11 = (bf16[96,1664]{1,0:T(8,128)(2,1)S(1)}, bf16[96,1664]{1,0:T(8,128)(2,1)S(1)}, u32[]{:S(2)}, u32[]{:S(2)}) collective-permute-start(bf16[96,1664]{1,0:T(8,128)(2,1)S(1)} %get-tuple-element.125), channel_id=1, source_target_pairs={{0,4},{1,5},{2,6},{3,7},{4,0},{5,1},{6,2},{7,3},{8,12},{9,13},{10,... | collective-permute-start | bytes 958472 | tf_op jit(solution)/shard_map/ppermute | solution.py:38
  152.7 9.2 %collective-permute-start.28 = (bf16[48,1536]{1,0:T(8,128)(2,1)S(1)}, bf16[48,1536]{1,0:T(8,128)(2,1)S(1)}, u32[]{:S(2)}, u32[]{:S(2)}) collective-permute-start(bf16[48,1536]{1,0:T(8,128)(2,1)S(1)} %get-tuple-element.147), channel_id=1, source_target_pairs={{0,8},{1,9},{2,10},{3,11},{4,12},{5,13},{6,14},{7,15},{8,0},{9,1},... | collective-permute-start | bytes 442376 | tf_op jit(solution)/shard_map/ppermute | solution.py:38
  161.9 33.2 %collective-permute-start.8 = (bf16[256,768]{1,0:T(8,128)(2,1)}, bf16[256,768]{1,0:T(8,128)(2,1)S(1)}, u32[]{:S(2)}, u32[]{:S(2)}) collective-permute-start(bf16[256,768]{1,0:T(8,128)(2,1)} %get-tuple-element.120), channel_id=1, source_target_pairs={{0,16},{16,0},{1,17},{17,1},{2,18},{18,2},{3,19},{19,3},{4,20},{20... | collective-permute-start | bytes 1179656 | tf_op jit(solution)/shard_map/ppermute | solution.py:33
  164.1 21.0 %collective-permute-start.25 = (bf16[48,1536]{1,0:T(8,128)(2,1)S(1)}, bf16[48,1536]{1,0:T(8,128)(2,1)S(1)}, u32[]{:S(2)}, u32[]{:S(2)}) collective-permute-start(bf16[48,1536]{1,0:T(8,128)(2,1)S(1)} %get-tuple-element.143), channel_id=1, source_target_pairs={{0,8},{1,9},{2,10},{3,11},{4,12},{5,13},{6,14},{7,15},{8,0},{9,1},... | collective-permute-start | bytes 442376 | tf_op jit(solution)/shard_map/ppermute | solution.py:38
  168.6 29.2 %collective-permute-start.21 = (bf16[96,1536]{1,0:T(8,128)(2,1)}, bf16[96,1536]{1,0:T(8,128)(2,1)}, u32[]{:S(2)}, u32[]{:S(2)}) collective-permute-start(bf16[96,1536]{1,0:T(8,128)(2,1)} %get-tuple-element.137), channel_id=1, source_target_pairs={{0,4},{1,5},{2,6},{3,7},{4,0},{5,1},{6,2},{7,3},{8,12},{9,13},{10,... | collective-permute-start | bytes 884744 | tf_op jit(solution)/shard_map/ppermute | solution.py:38
  180.9 18.5 %collective-permute-start.18 = (bf16[96,1536]{1,0:T(8,128)(2,1)}, bf16[96,1536]{1,0:T(8,128)(2,1)}, u32[]{:S(2)}, u32[]{:S(2)}) collective-permute-start(bf16[96,1536]{1,0:T(8,128)(2,1)} %get-tuple-element.133), channel_id=1, source_target_pairs={{0,4},{1,5},{2,6},{3,7},{4,0},{5,1},{6,2},{7,3},{8,12},{9,13},{10,... | collective-permute-start | bytes 884744 | tf_op jit(solution)/shard_map/ppermute | solution.py:38
  183.5 19.6 %collective-permute-start.15 = (bf16[96,1536]{1,0:T(8,128)(2,1)}, bf16[96,1536]{1,0:T(8,128)(2,1)}, u32[]{:S(2)}, u32[]{:S(2)}) collective-permute-start(bf16[96,1536]{1,0:T(8,128)(2,1)} %get-tuple-element.129), channel_id=1, source_target_pairs={{0,4},{1,5},{2,6},{3,7},{4,0},{5,1},{6,2},{7,3},{8,12},{9,13},{10,... | collective-permute-start | bytes 884744 | tf_op jit(solution)/shard_map/ppermute | solution.py:38
  185.8 18.7 %collective-permute-start.12 = (bf16[48,1664]{1,0:T(8,128)(2,1)}, bf16[48,1664]{1,0:T(8,128)(2,1)}, u32[]{:S(2)}, u32[]{:S(2)}) collective-permute-start(bf16[48,1664]{1,0:T(8,128)(2,1)} %get-tuple-element.127), channel_id=1, source_target_pairs={{0,8},{1,9},{2,10},{3,11},{4,12},{5,13},{6,14},{7,15},{8,0},{9,1},... | collective-permute-start | bytes 479240 | tf_op jit(solution)/shard_map/ppermute | solution.py:38
  195.1 10.7 %collective-permute-start.6 = (bf16[256,768]{1,0:T(8,128)(2,1)S(1)}, bf16[256,768]{1,0:T(8,128)(2,1)S(1)}, u32[]{:S(2)}, u32[]{:S(2)}) collective-permute-start(bf16[256,768]{1,0:T(8,128)(2,1)S(1)} %slice.50), channel_id=1, source_target_pairs={{0,16},{16,0},{1,17},{17,1},{2,18},{18,2},{3,19},{19,3},{4,20},{20... | collective-permute-start | bytes 1179656 | tf_op jit(solution)/shard_map/ppermute | solution.py:33
  198.9 15.9 %collective-permute-start.22 = (bf16[48,1536]{1,0:T(8,128)(2,1)S(1)}, bf16[48,1536]{1,0:T(8,128)(2,1)S(1)}, u32[]{:S(2)}, u32[]{:S(2)}) collective-permute-start(bf16[48,1536]{1,0:T(8,128)(2,1)S(1)} %get-tuple-element.139), channel_id=1, source_target_pairs={{0,8},{1,9},{2,10},{3,11},{4,12},{5,13},{6,14},{7,15},{8,0},{9,1},... | collective-permute-start | bytes 442376 | tf_op jit(solution)/shard_map/ppermute | solution.py:38
  200.4 17.6 %collective-permute-start.19 = (bf16[48,1536]{1,0:T(8,128)(2,1)S(1)}, bf16[48,1536]{1,0:T(8,128)(2,1)S(1)}, u32[]{:S(2)}, u32[]{:S(2)}) collective-permute-start(bf16[48,1536]{1,0:T(8,128)(2,1)S(1)} %get-tuple-element.135), channel_id=1, source_target_pairs={{0,8},{1,9},{2,10},{3,11},{4,12},{5,13},{6,14},{7,15},{8,0},{9,1},... | collective-permute-start | bytes 442376 | tf_op jit(solution)/shard_map/ppermute | solution.py:38
  204.1 16.6 %collective-permute-start.16 = (bf16[48,1536]{1,0:T(8,128)(2,1)S(1)}, bf16[48,1536]{1,0:T(8,128)(2,1)S(1)}, u32[]{:S(2)}, u32[]{:S(2)}) collective-permute-start(bf16[48,1536]{1,0:T(8,128)(2,1)S(1)} %get-tuple-element.131), channel_id=1, source_target_pairs={{0,8},{1,9},{2,10},{3,11},{4,12},{5,13},{6,14},{7,15},{8,0},{9,1},... | collective-permute-start | bytes 442376 | tf_op jit(solution)/shard_map/ppermute | solution.py:38
  205.5 16.3 %collective-permute-start.13 = (bf16[48,1664]{1,0:T(8,128)(2,1)S(1)}, bf16[48,1664]{1,0:T(8,128)(2,1)S(1)}, u32[]{:S(2)}, u32[]{:S(2)}) collective-permute-start(bf16[48,1664]{1,0:T(8,128)(2,1)S(1)} %get-tuple-element.154), channel_id=1, source_target_pairs={{0,16},{16,0},{1,17},{17,1},{2,18},{18,2},{3,19},{19,3},{4,20},{20... | collective-permute-start | bytes 479240 | tf_op jit(solution)/shard_map/ppermute | solution.py:33
  (39 other events, 276.9 us)
